TPU v7x, 256 devices: a whole 4x4x8 slice. The times are simulated.
256 devices in a mesh: dp: 16 (over y, x_hi, core), tensor: 16 (over z, x_lo).
Axes of the slice: x: 4 (x_hi: 2, x_lo: 2; x = x_hi * 2 + x_lo), y: 4, z: 8, core: 2. Of those that a mesh axis runs over, the one named last changes fastest.
Arguments:
- activations: bfloat16 [8192, 8192], P('dp'), may hold values from -6 to 6
- basis: bfloat16 [8192, 512], P('dp'), may hold values from -0.25 to 0.25
- out_grads: bfloat16 [8192, 28672], P('dp', 'tensor'), may hold values from -0.046875 to 0.046875
- first_moment: float32 [512, 28672], P('dp', 'tensor'), may hold values from -6 to 6
- second_moment: float32 [512, 28672], P('dp', 'tensor'), may hold values from 0.01 to 0.1
Outputs:
- weight_update: bfloat16 [8192, 28672], P('dp', 'tensor')
- new_first: float32 [512, 28672], P('dp', 'tensor')
- new_second: float32 [512, 28672], P('dp', 'tensor')
All inputs are finite; a program needn't handle non-finite values.
Results may differ from a plain program's by a relative error of at most 0.0051.
Values may be sent and summed in bfloat16 or wider, within the bound.
A program may use at most 64 MiB of HBM per device.

v0:
```python
import jax
import jax.numpy as jnp
from jax import lax
from jax.sharding import PartitionSpec as P

beta_one = 0.9
beta_two = 0.999
first_fix = 1.0 - 0.9**50
second_fix = 1.0 - 0.999**50
adam_eps = 1e-08


def on_device(activations, basis, out_grads, first_moment, second_moment):
    columns = activations
    summed = jnp.dot(
        columns, lax.all_gather(basis, "dp", axis=0, tiled=True), preferred_element_type=jnp.float32
    )
    projected = summed.astype(jnp.bfloat16)
    owned_rows = first_moment.shape[0]
    partial_grad = lax.dot_general(
        projected, out_grads, (((0,), (0,)), ((), ())), preferred_element_type=jnp.float32
    )
    total_grad = lax.psum(partial_grad, "dp")
    low_grad = lax.dynamic_slice_in_dim(
        total_grad, lax.axis_index("dp") * owned_rows, owned_rows, 0
    )
    new_first = beta_one * first_moment + (1.0 - beta_one) * low_grad
    new_second = beta_two * second_moment + (1.0 - beta_two) * low_grad * low_grad
    direction = (new_first / first_fix / (jnp.sqrt(new_second / second_fix) + adam_eps)).astype(
        jnp.bfloat16
    )
    columns = basis
    weight_update = jnp.dot(
        columns,
        lax.all_gather(direction, "dp", axis=0, tiled=True),
        preferred_element_type=jnp.float32,
    )
    return (weight_update.astype(jnp.bfloat16), new_first, new_second)


def solution(mesh):
    placed = (P("dp", None), P("dp", None), P("dp", "tensor"), P("dp", "tensor"), P("dp", "tensor"))
    return jax.shard_map(
        on_device,
        mesh=mesh,
        in_specs=placed,
        out_specs=(P("dp", "tensor"), P("dp", "tensor"), P("dp", "tensor")),
        check_vma=False,
    )
```

profile of v0, /device:TPU:1, one launch (start us, length us, event | category | flops | bytes accessed | tf_op | source)
XLA Modules:
  0.0 332.1 jit_solution(11952839826843410988)
XLA Ops:
  7.2 0.0 copy-start
  7.2 0.0 all-gather.3.cloned.1.call-start
  7.2 0.7 all-gather.3.cloned.1.call-update
  7.9 0.0 all-reduce.2.cloned.1.call-start
  8.0 85.1 %all-gather.3.cloned.1.call-done = bf16[8192,512]{1,0:T(8,128)(2,1)} async-done(((bf16[512,512]{1,0:T(8,128)(2,1)}), bf16[8192,512]{1,0:T(8,128)(2,1)}) %all-gather.3.cloned.1.call-update) | async-done | bytes 8388624 | tf_op jit(solution)/shard_map/all_gather | solution.py:16
  93.0 0.0 copy-done
  93.0 13.3 %fusion.1 = f32[512,1792]{1,0:T(8,128)} fusion(bf16[512,1792]{1,0:T(8,128)(2,1)S(1)} %copy-done, bf16[512,8192]{1,0:T(8,128)(2,1)} %param.5, bf16[8192,512]{1,0:T(8,128)(2,1)} %all-gather.3.cloned.1.call-done), kind=kOutput, calls=%fused_computation.3 | convolution fusion | flops 5234753536 | bytes 22282240 | tf_op jit(solution)/shard_map/dot_general | solution.py:20
  106.4 0.0 copy-start.2
  106.4 0.0 copy-start.3
  106.4 0.0 copy-start.1
  106.4 0.0 all-reduce.2.cloned.1.call-update
  106.4 0.0 all-gather.5.cloned.1.call-start
  106.5 154.4 %all-reduce.2.cloned.1.call-done = f32[512,1792]{1,0:T(8,128)} async-done(((f32[512,1792]{1,0:T(8,128)}), f32[512,1792]{1,0:T(8,128)}) %all-reduce.2.cloned.1.call-update) | async-done | bytes 3670032 | tf_op jit(solution)/shard_map/psum | solution.py:23
  260.9 0.0 copy-done.2
  260.9 0.0 copy-done.3
  260.9 1.8 divide_convert_fusion
  262.7 0.0 all-gather.5.cloned.1.call-update
  262.7 55.2 %all-gather.5.cloned.1.call-done = bf16[512,1792]{1,0:T(8,128)(2,1)} async-done(((bf16[32,1792]{1,0:T(8,128)(2,1)}), bf16[512,1792]{1,0:T(8,128)(2,1)}) %all-gather.5.cloned.1.call-update) | async-done | bytes 1835024 | tf_op jit(solution)/shard_map/all_gather | solution.py:35
  317.9 0.0 copy-done.1
  317.9 3.9 %fusion = bf16[512,1792]{0,1:T(8,128)(2,1)} fusion(bf16[512,1792]{1,0:T(8,128)(2,1)} %all-gather.5.cloned.1.call-done, bf16[512,512]{1,0:T(8,128)(2,1)S(1)} %copy-done.1), kind=kOutput, calls=%fused_computation.1 | convolution fusion | flops 940441600 | bytes 4194304 | tf_op jit(solution)/shard_map/dot_general | solution.py:33
  321.8 3.8 %copy.8 = bf16[512,1792]{1,0:T(8,128)(2,1)} copy(bf16[512,1792]{0,1:T(8,128)(2,1)} %fusion) | data formatting | bytes 3670016
Async XLA Ops:
  7.2 85.9 %copy-start = (bf16[512,1792]{1,0:T(8,128)(2,1)S(1)}, bf16[512,1792]{1,0:T(8,128)(2,1)}, u32[]{:S(2)}) copy-start(bf16[512,1792]{1,0:T(8,128)(2,1)} %param.7) | copy-start | bytes 5505028
  7.2 85.9 %all-gather.3.cloned.1.call-start = ((), (), s32[]{:S(2)}) async-start(), calls=%async_computation | async-start | bytes 8912896 | tf_op jit(solution)/shard_map/all_gather | solution.py:16
  7.9 253.0 %all-reduce.2.cloned.1.call-start = ((), (), s32[]{:S(2)}) async-start(), calls=%async_computation.1 | async-start | bytes 7340032 | tf_op jit(solution)/shard_map/psum | solution.py:23
  106.4 154.5 %copy-start.2 = (f32[32,1792]{1,0:T(8,128)S(1)}, f32[32,1792]{1,0:T(8,128)}, u32[]{:S(2)}) copy-start(f32[32,1792]{1,0:T(8,128)} %param.8) | copy-start | bytes 688132
  106.4 154.5 %copy-start.3 = (f32[32,1792]{1,0:T(8,128)S(1)}, f32[32,1792]{1,0:T(8,128)}, u32[]{:S(2)}) copy-start(f32[32,1792]{1,0:T(8,128)} %param.9) | copy-start | bytes 688132
  106.4 211.5 %copy-start.1 = (bf16[512,512]{1,0:T(8,128)(2,1)S(1)}, bf16[512,512]{1,0:T(8,128)(2,1)}, u32[]{:S(2)}) copy-start(bf16[512,512]{1,0:T(8,128)(2,1)} %param.6) | copy-start | bytes 1572868
  106.4 211.5 %all-gather.5.cloned.1.call-start = ((), (), s32[]{:S(2)}) async-start(), calls=%async_computation.2 | async-start | bytes 1949696 | tf_op jit(solution)/shard_map/all_gather | solution.py:35
Sparse Core Ops, SparseCore 0:
  10.8 82.2 all-gather.2
  106.5 154.3 all-reduce.1
  264.2 53.6 all-gather.4
where the time goes:
time: 332 us
  waiting for transfers between devices  295 us (89%)
  matrix products  17.2 us (5%)
  between operations  13.8 us (4%)
  local copies, waits for them, and re-layouts  3.82 us (1%)
    psum x1, waiting for transfers between devices, on_device(): total_grad = lax.psum(partial_grad, 'dp')  154 us
    all_gather x1, waiting for transfers between devices, on_device(): lax.all_gather(basis, 'dp', axis=0, tiled=True)  85.1 us
    all_gather x1, waiting for transfers between devices, on_device(): lax.all_gather(direction, 'dp', axis=0, tiled=True)  55.2 us
    dot_general x1, matrix products, on_device(): lax.dot_general(projected, out_grads, (((0,), (0,)), ((), ())), preferred...  13.3 us
  transfers between devices with their start and end apart: 3, of which 3 were waited for; matrix products, arithmetic and copies ran while one was open for 0% of the time, Pallas kernels for 0%

commit v1 on v0

v1 whole, which is shorter than its diff:
```python
import functools

import jax
import jax.numpy as jnp
from jax import lax
from jax.experimental import pallas as pl
from jax.experimental.pallas import tpu as pltpu
from jax.sharding import PartitionSpec as P

beta_one = 0.9
beta_two = 0.999
first_fix = 1.0 - 0.9**50
second_fix = 1.0 - 0.999**50
adam_eps = 1e-08

MESH = pl.DeviceIdType.MESH
bf16 = jnp.bfloat16
f32 = jnp.float32

CHIPS = 8
NEAR = ((1, 0), (3, 0), (0, 1), (2, 0), (1, 1), (3, 1), (2, 1))
AHEAD = (0, 1, 3, 2)


def drain(ref, sem):
    pltpu.make_async_copy(ref, ref, sem).wait()


def kernel(
    act, basis, grads, first, second,
    update, new_first, new_second,
    act_v, basis_v, grads_v, first_v, second_v,
    mixed_v, picked, proj, table, part, got, held, rows_v, total, update_v, first_o, second_o,
    in_sem, og_sem, a1_send, a1_recv, fw_send, fw_recv, sib_sem, a2_send, a2_recv,
    b_send, b_recv, c_send, c_recv, cs_recv, cf_send, cf_recv, out_sem,
):
    i, j = lax.axis_index("dp"), lax.axis_index("tensor")
    core, chip = i % 2, i // 2
    y, x = chip // 2, chip % 2
    quad, member = j // 4, j % 4
    depth = basis.shape[0]
    width = grads.shape[1]
    half = width // 2

    def chip_at(dy, dx):
        return ((y + dy) % 4) * 2 + (x + dx) % 2

    sibling = (2 * chip + (1 - core), j)
    peers = [(2 * dy + dx, chip_at(dy, dx)) for dy, dx in NEAR]

    loads = [pltpu.make_async_copy(basis, basis_v, in_sem.at[0])]
    loads.append(pltpu.make_async_copy(grads, grads_v.at[core], in_sem.at[1]))
    loads.append(pltpu.make_async_copy(first, first_v, in_sem.at[2]))
    loads.append(pltpu.make_async_copy(second, second_v, in_sem.at[3]))
    for load in loads:
        load.start()
    for b in range(16):
        pltpu.make_async_copy(act.at[:, pl.ds(b * depth, depth)], act_v.at[b], in_sem.at[4]).start()

    barrier = pltpu.get_barrier_semaphore()
    greeted = [sibling] + [(2 * q + core, j) for _, q in peers]
    for k, ahead in enumerate(AHEAD):
        for r in range(4):
            if k or r:
                greeted.append((i, 4 * ((quad + 4 - ahead) % 4) + (member + r) % 4))
    for device in greeted:
        pl.semaphore_signal(barrier, inc=1, device_id=device, device_id_type=MESH)

    loads[0].wait()
    r = lax.broadcasted_iota(jnp.int32, (32, 512), 0)
    col = lax.broadcasted_iota(jnp.int32, (32, 512), 1)
    owner = 2 * (2 * member + ((r >> 3) & 1)) + (r >> 4)
    pick = (col == 32 * owner + 8 * quad + (r & 7)).astype(bf16)
    nt = (((1,), (1,)), ((), ()))
    picked[0, 0] = lax.dot_general(pick, basis_v[...], nt, preferred_element_type=f32).astype(bf16)

    pl.semaphore_wait(barrier, len(greeted))

    for d, q in peers:
        pltpu.make_async_remote_copy(
            picked.at[0, 0], picked.at[0, d], a1_send, a1_recv.at[d], (2 * q + core, j), MESH
        ).start()
    pltpu.make_async_remote_copy(
        picked.at[0, 0], picked.at[1, 0], fw_send, fw_recv.at[0], sibling, MESH
    ).start()
    to_sibling = pltpu.make_async_remote_copy(
        grads, grads_v.at[core], og_sem.at[0], og_sem.at[1], sibling, MESH
    )
    to_sibling.start()

    row = lax.broadcasted_iota(jnp.int32, (512, 512), 0)
    s = lax.broadcasted_iota(jnp.int32, (512, 512), 1)
    kk, pr, d, r = s >> 8, (s >> 7) & 1, (s >> 4) & 7, s & 15
    from_y = (y + 4 - (d >> 1)) & 3
    from_x = (x + 2 - (d & 1)) & 1
    from_core = (core + pr) & 1
    k = 2 * kk + (r >> 3)
    ahead = jnp.where(k == 2, 3, jnp.where(k == 3, 2, k))
    col = 32 * (2 * (2 * from_y + from_x) + from_core) + 8 * ((quad + ahead) & 3) + (r & 7)
    mix = (row == col).astype(bf16)
    mixed_v[...] = jnp.dot(basis_v[...], mix, preferred_element_type=f32).astype(bf16)

    pltpu.make_async_copy(act_v, act_v, in_sem.at[4]).wait()

    def times(pr, d, dy, dx):
        from_chip = ((y + 4 - dy) % 4) * 2 + (x + 2 - dx) % 2
        block = 2 * from_chip + (core + pr) % 2
        return lax.dot_general(picked[pr, d], act_v[block], nt, preferred_element_type=f32)

    acc = times(0, 0, 0, 0)
    for dy, dx in NEAR:
        d = 2 * dy + dx
        drain(picked.at[0, d], a1_recv.at[d])
        pltpu.make_async_remote_copy(
            picked.at[0, d], picked.at[1, d], fw_send, fw_recv.at[d], sibling, MESH
        ).start()
        acc += times(0, d, dy, dx)
    for dy, dx in ((0, 0),) + NEAR:
        d = 2 * dy + dx
        drain(picked.at[1, d], fw_recv.at[d])
        acc += times(1, d, dy, dx)
    acc = acc.astype(bf16)
    proj[0] = acc[:16]
    proj[1] = acc[16:]

    swap = pltpu.make_async_remote_copy(
        proj.at[1 - core], table.at[0, member, core], sib_sem.at[0], sib_sem.at[1], sibling, MESH
    )
    swap.start()
    table[0, member, core] = proj[core]
    drain(table.at[0, member, 1 - core], sib_sem.at[1])
    for k, ahead in enumerate(AHEAD):
        for r in range(4):
            if k or r:
                target = 4 * ((quad + 4 - ahead) % 4) + (member + r) % 4
                pltpu.make_async_remote_copy(
                    table.at[0, member], table.at[k, member], a2_send.at[k], a2_recv.at[k],
                    (i, target), MESH,
                ).start()
    loads[1].wait()
    loads[2].wait()
    loads[3].wait()
    drain(grads_v.at[1 - core], og_sem.at[1])

    def partial(k):
        drain(table.at[k] if k else table.at[0, pl.ds(0, 3)], a2_recv.at[k])
        left = table[k, :, 0].reshape(64, depth)
        right = table[k, :, 1].reshape(64, depth)
        halves = []
        for h in range(2):
            cols = pl.ds(h * half, half)
            halves.append(
                jnp.dot(left, grads_v[0, :, cols], preferred_element_type=f32)
                + jnp.dot(right, grads_v[1, :, cols], preferred_element_type=f32)
            )
        for q in range(8):
            both = [v[8 * q : 8 * q + 8] for v in halves]
            part[k, q] = jnp.concatenate(both, axis=0).astype(bf16)
        for d, q in peers:
            pltpu.make_async_remote_copy(
                part.at[k, q], got.at[k, d - 1], b_send.at[k], b_recv.at[k], (2 * q + core, j), MESH
            ).start()

    def reduce(k):
        drain(got.at[k], b_recv.at[k])
        low = part[k, chip].astype(f32)
        for d in range(7):
            low += got[k, d].astype(f32)
        at = pl.ds(pl.multiple_of(8 * ((quad + AHEAD[k]) % 4), 8), 8)
        for h in range(2):
            cols = pl.ds(h * half, half)
            g = low[8 * h : 8 * h + 8]
            nf = beta_one * first_v[at, cols] + (1.0 - beta_one) * g
            ns = beta_two * second_v[at, cols] + (1.0 - beta_two) * g * g
            first_o[at, cols] = nf
            second_o[at, cols] = ns
            rows_v[pl.ds(8 * (k % 2), 8), cols] = nf / first_fix / (
                jnp.sqrt(ns / second_fix) + adam_eps
            )

    def spread(kk):
        held[kk, 0, 0] = rows_v[...].astype(bf16)
        for d, q in peers:
            pltpu.make_async_remote_copy(
                held.at[kk, 0, 0], held.at[kk, 0, d], c_send.at[kk], c_recv.at[kk],
                (2 * q + core, j), MESH,
            ).start()
        pltpu.make_async_remote_copy(
            held.at[kk, 0, 0], held.at[kk, 1, 0], cf_send.at[kk], cs_recv.at[kk], sibling, MESH
        ).start()

    def forward(kk):
        others = pl.ds(1, 7)
        drain(held.at[kk, 0, others], c_recv.at[kk])
        pltpu.make_async_remote_copy(
            held.at[kk, 0, others], held.at[kk, 1, others], cf_send.at[kk], cf_recv.at[kk],
            sibling, MESH,
        ).start()

    def arrived(kk):
        drain(held.at[kk, 1, 0], cs_recv.at[kk])
        drain(held.at[kk, 1, pl.ds(1, 7)], cf_recv.at[kk])

    partial(0)
    partial(1)
    reduce(0)
    partial(2)
    reduce(1)
    spread(0)
    partial(3)
    reduce(2)
    forward(0)
    reduce(3)
    spread(1)
    outs = [
        pltpu.make_async_copy(first_o, new_first, out_sem.at[0]),
        pltpu.make_async_copy(second_o, new_second, out_sem.at[1]),
    ]
    for out in outs:
        out.start()
    arrived(0)
    tiles = [pl.ds(t * 256, 256) for t in range(width // 256)]
    for cols in tiles:
        total[:, cols] = jnp.dot(
            mixed_v[:, pl.ds(0, 256)], held[0, :, :, :, cols].reshape(256, 256),
            preferred_element_type=f32,
        )
    forward(1)
    arrived(1)
    for t, cols in enumerate(tiles):
        last = jnp.dot(
            mixed_v[:, pl.ds(256, 256)], held[1, :, :, :, cols].reshape(256, 256),
            preferred_element_type=f32,
        )
        update_v[:, cols] = (total[:, cols] + last).astype(bf16)
        out = pltpu.make_async_copy(update_v.at[:, cols], update.at[:, cols], out_sem.at[2 + t])
        out.start()
        outs.append(out)

    drain(picked.at[0, pl.ds(0, 7)], a1_send)
    drain(picked.at[1], fw_send)
    drain(grads, og_sem.at[0])
    drain(proj.at[0], sib_sem.at[0])
    for k in range(4):
        drain(table.at[k] if k else table.at[0, pl.ds(0, 3)], a2_send.at[k])
        drain(got.at[k], b_send.at[k])
    for kk in range(2):
        drain(held.at[kk, 0, pl.ds(1, 7)], c_send.at[kk])
        drain(held.at[kk, 1], cf_send.at[kk])
    for out in outs:
        out.wait()


def on_device(act, basis, grads, first, second):
    tokens, depth = act.shape[0], basis.shape[0]
    rank, width = basis.shape[1], grads.shape[1]
    rows = first.shape[0]
    dma = pltpu.SemaphoreType.DMA
    anywhere = pl.BlockSpec(memory_space=pl.ANY)
    return pl.pallas_call(
        kernel,
        out_shape=(
            jax.ShapeDtypeStruct((depth, width), bf16),
            jax.ShapeDtypeStruct((rows, width), f32),
            jax.ShapeDtypeStruct((rows, width), f32),
        ),
        in_specs=[anywhere] * 5,
        out_specs=[anywhere] * 3,
        scratch_shapes=[
            pltpu.VMEM((16, tokens, depth), bf16),
            pltpu.VMEM((depth, rank), bf16),
            pltpu.VMEM((2, tokens, width), bf16),
            pltpu.VMEM((rows, width), f32),
            pltpu.VMEM((rows, width), f32),
            pltpu.VMEM((depth, rank), bf16),
            pltpu.VMEM((2, 8, 32, depth), bf16),
            pltpu.VMEM((2, 16, tokens), bf16),
            pltpu.VMEM((4, 4, 2, 16, tokens), bf16),
            pltpu.VMEM((4, 8, 16, width // 2), bf16),
            pltpu.VMEM((4, 7, 16, width // 2), bf16),
            pltpu.VMEM((2, 2, 8, 16, width), bf16),
            pltpu.VMEM((16, width), f32),
            pltpu.VMEM((depth, width), f32),
            pltpu.VMEM((depth, width), bf16),
            pltpu.VMEM((rows, width), f32),
            pltpu.VMEM((rows, width), f32),
            dma((5,)), dma((2,)), dma, dma((8,)), dma, dma((8,)), dma((2,)), dma((4,)), dma((4,)),
            dma((4,)), dma((4,)), dma((2,)), dma((2,)), dma((2,)), dma((2,)), dma((2,)),
            dma((2 + width // 256,)),
        ],
        compiler_params=pltpu.CompilerParams(
            collective_id=0, has_side_effects=True, vmem_limit_bytes=48 << 20
        ),
    )(act, basis, grads, first, second)


def solution(mesh):
    placed = (P("dp", None), P("dp", None), P("dp", "tensor"), P("dp", "tensor"), P("dp", "tensor"))
    return jax.shard_map(
        on_device,
        mesh=mesh,
        in_specs=placed,
        out_specs=(P("dp", "tensor"), P("dp", "tensor"), P("dp", "tensor")),
        check_vma=False,
    )
```

time: 332 us -> 68.5 us (0.21)
  waiting for transfers between devices: 295 us -> 0 us
  Pallas kernels: 0 us -> 59.6 us
  matrix products: 17.2 us -> 0 us
  between operations: 13.8 us -> 0.65 us
    psum x1 -> x0, waiting for transfers between devices: 154 us -> none  [on_device(): total_grad = lax.psum(partial_grad, 'dp')]
    all_gather x2 -> x0, waiting for transfers between devices: 140 us -> none  [the longest x1 85.1 us: on_device(): lax.all_gather(basis, 'dp', axis=0, tiled=True)]
    pallas_call x0 -> x1, Pallas kernels: none -> 59.6 us  [on_device(): pl.pallas_call(kernel, out_shape=(jax.ShapeDtypeStruct((depth, width), bf...]
    dot_general x2 -> x0, matrix products: 17.2 us -> none  [the longest x1 13.3 us: on_device(): lax.dot_general(projected, out_grads, (((0,), (0,)), ((), ())), preferred...]
    unnamed x9 -> x11, local copies, waits for them, and re-layouts: 3.82 us -> 7.02 us
  transfers between devices with their start and end apart: 3 -> 0, of which waited for: 3 -> 0; matrix products, arithmetic and copies ran while one was open for 0% -> 0% of each run, Pallas kernels for 0% -> 0%
where the time goes in v1:
time: 68.5 us; the launch traced here: 67.2 us
  Pallas kernels  59.6 us (87%)
  local copies, waits for them, and re-layouts  7.02 us (10%)
    pallas_call x1, Pallas kernels, on_device(): pl.pallas_call(kernel, out_shape=(jax.ShapeDtypeStruct((depth, width), bf...  59.6 us
    unnamed x11, local copies, waits for them, and re-layouts  7.02 us

profile of v1, /device:TPU:1, one launch (start us, length us, event | category | flops | bytes accessed | tf_op | source)
XLA Modules:
  0.0 67.2 jit_solution(10196681087358473470)
XLA Ops:
  0.6 0.0 copy-start
  0.6 1.5 %copy-done = bf16[512,1792]{1,0:T(8,128)(2,1)S(1)} copy-done((bf16[512,1792]{1,0:T(8,128)(2,1)S(1)}, bf16[512,1792]{1,0:T(8,128)(2,1)}, u32[]{:S(2)}) %copy-start) | copy-done | bytes 1835032
  2.1 0.0 copy-start.1
  2.1 1.0 %copy-done.1 = bf16[512,512]{1,0:T(8,128)(2,1)S(1)} copy-done((bf16[512,512]{1,0:T(8,128)(2,1)S(1)}, bf16[512,512]{1,0:T(8,128)(2,1)}, u32[]{:S(2)}) %copy-start.1) | copy-done | bytes 524312
  3.2 0.0 copy-start.2
  3.2 0.9 %copy-done.2 = f32[32,1792]{1,0:T(8,128)S(1)} copy-done((f32[32,1792]{1,0:T(8,128)S(1)}, f32[32,1792]{1,0:T(8,128)}, u32[]{:S(2)}) %copy-start.2) | copy-done | bytes 229400
  4.1 0.0 copy-start.3
  4.1 0.9 %copy-done.3 = f32[32,1792]{1,0:T(8,128)S(1)} copy-done((f32[32,1792]{1,0:T(8,128)S(1)}, f32[32,1792]{1,0:T(8,128)}, u32[]{:S(2)}) %copy-start.3) | copy-done | bytes 229400
  5.1 59.6 %shard_map.76 = (bf16[512,1792]{1,0:T(8,128)(2,1)S(1)}, f32[32,1792]{1,0:T(8,128)S(1)}, f32[32,1792]{1,0:T(8,128)S(1)}) custom-call(bf16[512,8192]{1,0:T(8,128)(2,1)} %act.1, bf16[512,512]{1,0:T(8,128)(2,1)S(1)} %copy-done.1, bf16[512,1792]{1,0:T(8,128)(2,1)S(1)} %copy-done, f32[32,1792]{1,0:T(8,128)S(1)} %copy-done.2, f32[32,1792]{1,0:T(8,128)S(1)} %copy-done.3), custom_call_target="tpu_custom_call" | custom-call | tf_op jit(solution)/shard_map/pallas_call | solution.py:260
  64.6 1.2 %copy.11 = bf16[512,1792]{1,0:T(8,128)(2,1)} copy(bf16[512,1792]{1,0:T(8,128)(2,1)S(1)} %get-tuple-element.6) | data formatting | bytes 3670016
  65.9 0.7 %copy.12 = f32[32,1792]{1,0:T(8,128)} copy(f32[32,1792]{1,0:T(8,128)S(1)} %get-tuple-element.7) | data formatting | bytes 458752
  66.5 0.7 %copy.13 = f32[32,1792]{1,0:T(8,128)} copy(f32[32,1792]{1,0:T(8,128)S(1)} %get-tuple-element.8) | data formatting | bytes 458752
Async XLA Ops:
  0.6 1.5 %copy-start = (bf16[512,1792]{1,0:T(8,128)(2,1)S(1)}, bf16[512,1792]{1,0:T(8,128)(2,1)}, u32[]{:S(2)}) copy-start(bf16[512,1792]{1,0:T(8,128)(2,1)} %grads.1) | copy-start | bytes 5505028
  2.1 1.0 %copy-start.1 = (bf16[512,512]{1,0:T(8,128)(2,1)S(1)}, bf16[512,512]{1,0:T(8,128)(2,1)}, u32[]{:S(2)}) copy-start(bf16[512,512]{1,0:T(8,128)(2,1)} %basis.1) | copy-start | bytes 1572868
  3.2 0.9 %copy-start.2 = (f32[32,1792]{1,0:T(8,128)S(1)}, f32[32,1792]{1,0:T(8,128)}, u32[]{:S(2)}) copy-start(f32[32,1792]{1,0:T(8,128)} %first.1) | copy-start | bytes 688132
  4.1 0.9 %copy-start.3 = (f32[32,1792]{1,0:T(8,128)S(1)}, f32[32,1792]{1,0:T(8,128)}, u32[]{:S(2)}) copy-start(f32[32,1792]{1,0:T(8,128)} %second.1) | copy-start | bytes 688132

commit v2 on v0

v2 whole, which is shorter than its diff:
```python
import jax
import jax.numpy as jnp
from jax import lax
from jax.experimental import pallas as pl
from jax.experimental.pallas import tpu as pltpu
from jax.sharding import PartitionSpec as P

beta_one = 0.9
beta_two = 0.999
first_fix = 1.0 - 0.9**50
second_fix = 1.0 - 0.999**50
adam_eps = 1e-08

MESH = pl.DeviceIdType.MESH
bf16 = jnp.bfloat16
f32 = jnp.float32
scope = jax.named_scope

NEAR = ((1, 0), (3, 0), (0, 1), (2, 0), (1, 1), (3, 1), (2, 1))
AHEAD = (0, 1, 3, 2)
NT = (((1,), (1,)), ((), ()))


def drain(ref, sem):
    pltpu.make_async_copy(ref, ref, sem).wait()


def exchange(
    act, basis, grads, first, second,
    held, mixed, first_o, second_o,
    act_v, basis_v, grads_v, first_v, second_v,
    mixed_v, picked, proj, table, part, got, send_v, new_first, new_second,
    in_sem, og_sem, a1_send, a1_recv, fw_send, fw_recv, sib_sem, a2_send, a2_recv,
    b_send, b_recv, c_send, c_recv, cs_recv, cf_send, cf_recv, out_sem,
):
    i, j = lax.axis_index("dp"), lax.axis_index("tensor")
    core, chip = i % 2, i // 2
    y, x = chip // 2, chip % 2
    quad, member = j // 4, j % 4
    depth = basis.shape[0]
    half = grads.shape[1] // 2
    twin = 2 * chip + (1 - core)

    sibling = (twin, j)
    peers = [(2 * dy + dx, ((y + dy) % 4) * 2 + (x + dx) % 2) for dy, dx in NEAR]

    barrier = pltpu.get_barrier_semaphore()
    greeted = [sibling] + [(2 * q + core, j) for _, q in peers]
    for k, ahead in enumerate(AHEAD):
        for r in range(4):
            if k or r:
                greeted.append((i, 4 * ((quad + 4 - ahead) % 4) + (member + r) % 4))
    for r in range(1, 4):
        greeted.append((twin, 4 * quad + (member + r) % 4))
    for device in greeted:
        pl.semaphore_signal(barrier, inc=1, device_id=device, device_id_type=MESH)

    loads = [
        pltpu.make_async_copy(basis, basis_v, in_sem.at[0]),
        pltpu.make_async_copy(grads, grads_v.at[core], in_sem.at[1]),
        pltpu.make_async_copy(first, first_v, in_sem.at[2]),
        pltpu.make_async_copy(second, second_v, in_sem.at[3]),
    ]
    loads[0].start()
    for b in range(16):
        pltpu.make_async_copy(act.at[:, pl.ds(b * depth, depth)], act_v.at[b], in_sem.at[4]).start()
    for load in loads[1:]:
        load.start()

    loads[0].wait()
    r = lax.broadcasted_iota(jnp.int32, (32, 512), 0)
    col = lax.broadcasted_iota(jnp.int32, (32, 512), 1)
    owner = 2 * (2 * member + ((r >> 3) & 1)) + (r >> 4)
    pick = (col == 32 * owner + 8 * quad + (r & 7)).astype(bf16)
    picked[0, 0] = lax.dot_general(pick, basis_v[...], NT, preferred_element_type=f32).astype(bf16)

    with scope("greet"):
        pl.semaphore_wait(barrier, len(greeted))

    with scope("send_columns"):
        for d, q in peers:
            pltpu.make_async_remote_copy(
                picked.at[0, 0], picked.at[0, d], a1_send, a1_recv.at[d], (2 * q + core, j), MESH
            ).start()
        pltpu.make_async_remote_copy(
            picked.at[0, 0], picked.at[1, 0], fw_send, fw_recv.at[0], sibling, MESH
        ).start()
        pltpu.make_async_remote_copy(
            grads, grads_v.at[core], og_sem.at[0], og_sem.at[1], sibling, MESH
        ).start()

    with scope("reorder_basis"):
        row = lax.broadcasted_iota(jnp.int32, (512, 512), 0)
        s = lax.broadcasted_iota(jnp.int32, (512, 512), 1)
        k, pr, d, r = s >> 7, (s >> 6) & 1, (s >> 3) & 7, s & 7
        from_y = (y + 4 - (d >> 1)) & 3
        from_x = (x + 2 - (d & 1)) & 1
        from_core = (core + pr) & 1
        ahead = jnp.where(k == 2, 3, jnp.where(k == 3, 2, k))
        col = 32 * (2 * (2 * from_y + from_x) + from_core) + 8 * ((quad + ahead) & 3) + r
        mix = (row == col).astype(bf16)
        mixed_v[...] = jnp.dot(basis_v[...], mix, preferred_element_type=f32).astype(bf16)
        mixed_out = pltpu.make_async_copy(mixed_v, mixed, out_sem.at[0])
        mixed_out.start()

    with scope("act_wait"):
        pltpu.make_async_copy(act_v, act_v, in_sem.at[4]).wait()

    def times(pr, dy, dx):
        from_chip = ((y + 4 - dy) % 4) * 2 + (x + 2 - dx) % 2
        block = 2 * from_chip + (core + pr) % 2
        return lax.dot_general(
            picked[pr, 2 * dy + dx], act_v[block], NT, preferred_element_type=f32
        )

    def from_sibling(acc, dy, dx):
        with scope("sibling_columns"):
            drain(picked.at[1, 2 * dy + dx], fw_recv.at[2 * dy + dx])
        return acc + times(1, dy, dx)

    behind = ((0, 0),) + NEAR
    acc = times(0, 0, 0)
    for t, (dy, dx) in enumerate(NEAR):
        d = 2 * dy + dx
        with scope("columns%d" % t):
            drain(picked.at[0, d], a1_recv.at[d])
        pltpu.make_async_remote_copy(
            picked.at[0, d], picked.at[1, d], fw_send, fw_recv.at[d], sibling, MESH
        ).start()
        acc += times(0, dy, dx)
        if t:
            acc = from_sibling(acc, *behind[t - 1])
    acc = from_sibling(acc, *behind[6])
    acc = from_sibling(acc, *behind[7])
    acc = acc.astype(bf16)
    proj[0] = acc[:16]
    proj[1] = acc[16:]

    with scope("send_projected"):
        pltpu.make_async_remote_copy(
            proj.at[1 - core], table.at[0, member, core], sib_sem.at[0], sib_sem.at[1], sibling, MESH
        ).start()
        for r in range(1, 4):
            target = 4 * quad + (member + r) % 4
            for to_core, to_dp in ((core, i), (1 - core, twin)):
                pltpu.make_async_remote_copy(
                    proj.at[to_core], table.at[0, member, core], a2_send.at[0], a2_recv.at[0],
                    (to_dp, target), MESH,
                ).start()
        table[0, member, core] = proj[core]
        drain(table.at[0, member, 1 - core], sib_sem.at[1])
        for k, ahead in enumerate(AHEAD):
            for r in range(4):
                if k:
                    target = 4 * ((quad + 4 - ahead) % 4) + (member + r) % 4
                    pltpu.make_async_remote_copy(
                        table.at[0, member], table.at[k, member], a2_send.at[k], a2_recv.at[k],
                        (i, target), MESH,
                    ).start()
    for load in loads[1:]:
        load.wait()
    drain(grads_v.at[1 - core], og_sem.at[1])

    def partial(k):
        with scope("wait_projected%d" % k):
            drain(table.at[k] if k else table.at[0, pl.ds(0, 3)], a2_recv.at[k])
        with scope("partial%d" % k):
            left = table[k, :, 0].reshape(64, depth)
            right = table[k, :, 1].reshape(64, depth)
            halves = []
            for h in range(2):
                cols = pl.ds(h * half, half)
                halves.append(
                    jnp.dot(left, grads_v[0, :, cols], preferred_element_type=f32)
                    + jnp.dot(right, grads_v[1, :, cols], preferred_element_type=f32)
                )
            for q in range(8):
                both = [v[8 * q : 8 * q + 8] for v in halves]
                part[k, q] = jnp.concatenate(both, axis=0).astype(bf16)
            for d, q in peers:
                pltpu.make_async_remote_copy(
                    part.at[k, q], got.at[k, d - 1], b_send.at[k], b_recv.at[k],
                    (2 * q + core, j), MESH,
                ).start()

    def reduce(k):
        with scope("wait_sums%d" % k):
            drain(got.at[k], b_recv.at[k])
        with scope("adam%d" % k):
            low = part[k, chip].astype(f32)
            for d in range(7):
                low += got[k, d].astype(f32)
            at = pl.ds(pl.multiple_of(8 * ((quad + AHEAD[k]) % 4), 8), 8)
            rows = []
            for h in range(2):
                cols = pl.ds(h * half, half)
                g = low[8 * h : 8 * h + 8]
                nf = beta_one * first_v[at, cols] + (1.0 - beta_one) * g
                ns = beta_two * second_v[at, cols] + (1.0 - beta_two) * g * g
                new_first[at, cols] = nf
                new_second[at, cols] = ns
                rows.append(nf / first_fix / (jnp.sqrt(ns / second_fix) + adam_eps))
            send_v[k] = jnp.concatenate(rows, axis=0).astype(bf16)
            for d, q in peers:
                pltpu.make_async_remote_copy(
                    send_v.at[k], held.at[k, 0, d], c_send.at[k], c_recv.at[k],
                    (2 * q + core, j), MESH,
                ).start()
            pltpu.make_async_remote_copy(
                send_v.at[k], held.at[k, 1, 0], cf_send.at[k], cs_recv.at[k], sibling, MESH
            ).start()
            pltpu.make_async_copy(send_v.at[k], held.at[k, 0, 0], out_sem.at[1]).start()

    def forward(k):
        others = pl.ds(1, 7)
        with scope("wait_rows%d" % k):
            drain(held.at[k, 0, others], c_recv.at[k])
        pltpu.make_async_remote_copy(
            held.at[k, 0, others], held.at[k, 1, others], cf_send.at[k], cf_recv.at[k],
            sibling, MESH,
        ).start()


    partial(0)
    partial(1)
    reduce(0)
    partial(2)
    reduce(1)
    partial(3)
    reduce(2)
    reduce(3)
    outs = [
        mixed_out,
        pltpu.make_async_copy(new_first, first_o, out_sem.at[2]),
        pltpu.make_async_copy(new_second, second_o, out_sem.at[3]),
    ]
    for out in outs[1:]:
        out.start()
    for k in range(4):
        forward(k)

    drain(picked.at[0, pl.ds(0, 7)], a1_send)
    drain(picked.at[1], fw_send)
    drain(grads, og_sem.at[0])
    drain(proj.at[0], sib_sem.at[0])
    for k in range(4):
        drain(table.at[k] if k else table.at[0, pl.ds(0, 3)], a2_send.at[k])
        drain(got.at[k], b_send.at[k])
        drain(held.at[k, 0, pl.ds(1, 7)], c_send.at[k])
        drain(held.at[k, 1], cf_send.at[k])
    for out in outs:
        out.wait()
    drain(send_v, out_sem.at[1])
    with scope("wait_sibling_rows"):
        for k in range(4):
            drain(held.at[k, 1, 0], cs_recv.at[k])
            drain(held.at[k, 1, pl.ds(1, 7)], cf_recv.at[k])


def finish(held, mixed, first_i, second_i, update, first_o, second_o, rows_v, update_v, sem):
    outs = [
        pltpu.make_async_copy(first_i, first_o, sem.at[0]),
        pltpu.make_async_copy(second_i, second_o, sem.at[1]),
    ]
    for out in outs:
        out.start()
    width = update.shape[1]
    half = width // 2
    done = 0
    for h in range(2):
        for k in range(4):
            rows = held[k].reshape(16, 16, half).astype(f32)[:, 8 * h : 8 * h + 8]
            rows_v[128 * k : 128 * k + 128, pl.ds(h * half, half)] = rows.reshape(128, half).astype(bf16)
        while done < width and done + 256 <= (h + 1) * half:
            cols = pl.ds(done, 256)
            update_v[:, cols] = jnp.dot(
                mixed[...], rows_v[:, cols], preferred_element_type=f32
            ).astype(bf16)
            out = pltpu.make_async_copy(update_v.at[:, cols], update.at[:, cols], sem.at[2 + done // 256])
            out.start()
            outs.append(out)
            done += 256
    for out in outs:
        out.wait()


def on_device(act, basis, grads, first, second):
    tokens, depth = act.shape[0], basis.shape[0]
    rank, width = basis.shape[1], grads.shape[1]
    rows = first.shape[0]
    half = width // 2
    dma = pltpu.SemaphoreType.DMA
    anywhere = pl.BlockSpec(memory_space=pl.ANY)
    in_vmem = pl.BlockSpec(memory_space=pltpu.VMEM)
    operands = [pltpu.with_memory_space_constraint(v, pltpu.HBM) for v in (act, basis, grads, first, second)]
    held, mixed, new_first, new_second = pl.pallas_call(
        exchange,
        out_shape=(
            pltpu.VMEM((4, 2, 8, 16, half), bf16),
            pltpu.VMEM((depth, rank), bf16),
            pltpu.VMEM((rows, width), f32),
            pltpu.VMEM((rows, width), f32),
        ),
        in_specs=[anywhere] * 5,
        out_specs=[anywhere] * 4,
        scratch_shapes=[
            pltpu.VMEM((16, tokens, depth), bf16),
            pltpu.VMEM((depth, rank), bf16),
            pltpu.VMEM((2, tokens, width), bf16),
            pltpu.VMEM((rows, width), f32),
            pltpu.VMEM((rows, width), f32),
            pltpu.VMEM((depth, rank), bf16),
            pltpu.VMEM((2, 8, 32, depth), bf16),
            pltpu.VMEM((2, 16, tokens), bf16),
            pltpu.VMEM((4, 4, 2, 16, tokens), bf16),
            pltpu.VMEM((4, 8, 16, half), bf16),
            pltpu.VMEM((4, 7, 16, half), bf16),
            pltpu.VMEM((4, 16, half), bf16),
            pltpu.VMEM((rows, width), f32),
            pltpu.VMEM((rows, width), f32),
            dma((5,)), dma((2,)), dma, dma((8,)), dma, dma((8,)), dma((2,)), dma((4,)), dma((4,)),
            dma((4,)), dma((4,)), dma((4,)), dma((4,)), dma((4,)), dma((4,)), dma((4,)),
            dma((4,)),
        ],
        compiler_params=pltpu.CompilerParams(
            collective_id=0, has_side_effects=True, vmem_limit_bytes=32 << 20
        ),
    )(*operands)
    return pl.pallas_call(
        finish,
        out_shape=(
            pltpu.HBM((depth, width), bf16),
            pltpu.HBM((rows, width), f32),
            pltpu.HBM((rows, width), f32),
        ),
        in_specs=[in_vmem, in_vmem, anywhere, anywhere],
        out_specs=[anywhere] * 3,
        scratch_shapes=[
            pltpu.VMEM((rank, width), bf16),
            pltpu.VMEM((depth, width), bf16),
            dma((2 + width // 256,)),
        ],
        compiler_params=pltpu.CompilerParams(vmem_limit_bytes=24 << 20),
    )(held, mixed, new_first, new_second)


def solution(mesh):
    placed = (P("dp", None), P("dp", None), P("dp", "tensor"), P("dp", "tensor"), P("dp", "tensor"))
    return jax.shard_map(
        on_device,
        mesh=mesh,
        in_specs=placed,
        out_specs=(P("dp", "tensor"), P("dp", "tensor"), P("dp", "tensor")),
        check_vma=False,
    )
```

time: 332 us -> 57.7 us (0.17)
  waiting for transfers between devices: 295 us -> 0 us
  Pallas kernels: 0 us -> 56.9 us
  matrix products: 17.2 us -> 0 us
  between operations: 13.8 us -> 0.64 us
  local copies, waits for them, and re-layouts: 3.82 us -> 0 us
    psum x1 -> x0, waiting for transfers between devices: 154 us -> none  [on_device(): total_grad = lax.psum(partial_grad, 'dp')]
    all_gather x2 -> x0, waiting for transfers between devices: 140 us -> none  [the longest x1 85.1 us: on_device(): lax.all_gather(basis, 'dp', axis=0, tiled=True)]
    pallas_call x0 -> x2, Pallas kernels: none -> 56.9 us  [the longest x1 54.8 us: on_device(): pl.pallas_call(exchange, out_shape=(pltpu.VMEM((4, 2, 8, 16, half), bf16)...]
    dot_general x2 -> x0, matrix products: 17.2 us -> none  [the longest x1 13.3 us: on_device(): lax.dot_general(projected, out_grads, (((0,), (0,)), ((), ())), preferred...]
    unnamed x9 -> x0, local copies, waits for them, and re-layouts: 3.82 us -> none
  transfers between devices with their start and end apart: 3 -> 0, of which waited for: 3 -> 0; matrix products, arithmetic and copies ran while one was open for 0% -> 0% of each run, Pallas kernels for 0% -> 0%
where the time goes in v2:
time: 57.7 us; the launch traced here: 57.6 us
  Pallas kernels  56.9 us (99%)
  between operations  0.64 us (1%)
    pallas_call x1, Pallas kernels, on_device(): pl.pallas_call(exchange, out_shape=(pltpu.VMEM((4, 2, 8, 16, half), bf16)...  54.8 us
    pallas_call x1, Pallas kernels, on_device(): pl.pallas_call(finish, out_shape=(pltpu.HBM((depth, width), bf16), pltpu....  2.08 us

profile of v2, /device:TPU:1, one launch (start us, length us, event | category | flops | bytes accessed | tf_op | source)
XLA Modules:
  0.0 57.6 jit_solution(13843345118752252754)
XLA Ops:
  0.6 54.8 %shard_map.76 = (bf16[4,2,8,16,896]{4,3,2,1,0:T(8,128)(2,1)S(1)}, bf16[512,512]{1,0:T(8,128)(2,1)S(1)}, f32[32,1792]{1,0:T(8,128)S(1)}, f32[32,1792]{1,0:T(8,128)S(1)}) custom-call(bf16[512,8192]{1,0:T(8,128)(2,1)} %act.1, bf16[512,512]{1,0:T(8,128)(2,1)} %basis.1, bf16[512,1792]{1,0:T(8,128)(2,1)} %grads.1, f32[32,1792]{1,0:T(8,128)} %first.1, ...), custom_call_target="tpu_custom_call" | custom-call | tf_op jit(solution)/shard_map/pallas_call | solution.py:296
  55.5 2.1 %shard_map.77 = (bf16[512,1792]{1,0:T(8,128)(2,1)}, f32[32,1792]{1,0:T(8,128)}, f32[32,1792]{1,0:T(8,128)}) custom-call(bf16[4,2,8,16,896]{4,3,2,1,0:T(8,128)(2,1)S(1)} %get-tuple-element.7.held, bf16[512,512]{1,0:T(8,128)(2,1)S(1)} %get-tuple-element.8.mixed, f32[32,1792]{1,0:T(8,128)S(1)} %get-tuple-element.9.first_i, ...), custom_call_target="tpu_custom_call" | custom-call | tf_op jit(solution)/shard_map/pallas_call | solution.py:329

commit v3 on v2

v3 whole, which is shorter than its diff:
```python
import jax
import jax.numpy as jnp
from jax import lax
from jax.experimental import pallas as pl
from jax.experimental.pallas import tpu as pltpu
from jax.sharding import PartitionSpec as P

beta_one = 0.9
beta_two = 0.999
first_fix = 1.0 - 0.9**50
second_fix = 1.0 - 0.999**50
adam_eps = 1e-08

MESH = pl.DeviceIdType.MESH
bf16 = jnp.bfloat16
f32 = jnp.float32
scope = jax.named_scope

NEAR = ((1, 0), (3, 0), (0, 1), (2, 0), (1, 1), (3, 1), (2, 1))
ALL = ((0, 0),) + NEAR
RELAY = ("y then x", "x then y", "y then x", None)
NT = (((1,), (1,)), ((), ()))


def drain(ref, sem):
    pltpu.make_async_copy(ref, ref, sem).wait()


def slot_sem(d):
    return 0 if d < 4 else 1 if d == 4 else 2


def exchange(
    act, basis, grads, first, second,
    held, mixed, first_o, second_o,
    act_v, basis_v, grads_v, first_v, second_v,
    mixed_v, picked, proj, table, part, got, send_v, total, new_first, new_second,
    in_sem, og_sem, a1_send, a1_recv, fw_send, fw_recv, sib_sem, a2_send, a2_recv,
    b_send, b_recv, c_send, c_recv, cs_recv, cf_send, cf_recv, out_sem,
):
    i, j = lax.axis_index("dp"), lax.axis_index("tensor")
    core, chip = i % 2, i // 2
    y, x = chip // 2, chip % 2
    z, lo = j // 2, j % 2
    pair, odd = (z // 2) % 2, z % 2
    member = 2 * odd + lo
    depth = basis.shape[0]
    half = grads.shape[1] // 2
    twin = 2 * chip + (1 - core)

    sibling = (twin, j)
    peers = [(4 * dx + dy, ((y + dy) % 4) * 2 + (x + dx) % 2) for dy, dx in NEAR]
    by_slot = dict(peers)

    loads = [
        pltpu.make_async_copy(basis, basis_v, in_sem.at[0]),
        pltpu.make_async_copy(grads, grads_v.at[core], in_sem.at[1]),
        pltpu.make_async_copy(first, first_v, in_sem.at[2]),
        pltpu.make_async_copy(second, second_v, in_sem.at[3]),
    ]
    loads[0].start()

    barrier = pltpu.get_barrier_semaphore()
    def at(dz, to_lo):
        return 2 * ((z + 8 + dz) % 8) + to_lo

    mates = [at(0, 1 - lo), at(1 - 2 * odd, 0), at(1 - 2 * odd, 1)]
    next_z, across = 2 * odd - 1, 4 * lo - 2
    greeted = [sibling] + [(2 * q + core, j) for _, q in peers]
    greeted += [(to_dp, mate) for mate in mates for to_dp in (i, twin)]
    greeted += [(i, at(next_z, 0)), (i, at(next_z, 1)), (i, at(2, 0)), (i, at(-2, 1))]
    for device in greeted:
        pl.semaphore_signal(barrier, inc=1, device_id=device, device_id_type=MESH)

    loads[0].wait()
    r = lax.broadcasted_iota(jnp.int32, (64, 512), 0)
    col = lax.broadcasted_iota(jnp.int32, (64, 512), 1)
    owner = 2 * (2 * member + ((r >> 3) & 1)) + ((r >> 4) & 1)
    pick = (col == 32 * owner + 8 * (2 * (r >> 5) + pair) + (r & 7)).astype(bf16)
    both = lax.dot_general(pick, basis_v[...], NT, preferred_element_type=f32).astype(bf16)
    picked[0, 0, 0] = both[:32]
    picked[1, 0, 0] = both[32:]

    with scope("greet"):
        pl.semaphore_wait(barrier, len(greeted))

    def send_columns(t):
        with scope("send_columns%d" % t):
            for d, q in peers:
                pltpu.make_async_remote_copy(
                    picked.at[t, 0, 0], picked.at[t, 0, d], a1_send.at[t], a1_recv.at[8 if t else d],
                    (2 * q + core, j), MESH,
                ).start()
            pltpu.make_async_remote_copy(
                picked.at[t, 0, 0], picked.at[t, 1, 0], fw_send.at[t], fw_recv.at[8 * t], sibling, MESH
            ).start()

    send_columns(0)
    for b in range(16):
        pltpu.make_async_copy(act.at[:, pl.ds(b * depth, depth)], act_v.at[b], in_sem.at[4]).start()
    for load in loads[1:]:
        load.start()
    pltpu.make_async_remote_copy(
        grads, grads_v.at[core], og_sem.at[0], og_sem.at[1], sibling, MESH
    ).start()

    with scope("reorder_basis"):
        row = lax.broadcasted_iota(jnp.int32, (512, 512), 0)
        s = lax.broadcasted_iota(jnp.int32, (512, 512), 1)
        k, pr, d, r = s >> 7, (s >> 6) & 1, (s >> 3) & 7, s & 7
        from_y = (y + 4 - (d & 3)) & 3
        from_x = (x + 2 - (d >> 2)) & 1
        from_core = (core + pr) & 1
        block = 2 * (k >> 1) + ((pair + k) & 1)
        col = 32 * (2 * (2 * from_y + from_x) + from_core) + 8 * block + r
        mix = (row == col).astype(bf16)
        mixed_v[...] = jnp.dot(basis_v[...], mix, preferred_element_type=f32).astype(bf16)
        mixed_out = pltpu.make_async_copy(mixed_v, mixed, out_sem.at[0])
        mixed_out.start()

    with scope("act_wait"):
        pltpu.make_async_copy(act_v, act_v, in_sem.at[4]).wait()

    def partial(k):
        with scope("wait_projected%d" % k):
            drain(table.at[k] if k % 2 else table.at[k, pl.ds(0, 3)], a2_recv.at[k])
        with scope("partial%d" % k):
            left = table[k, :, 0].reshape(64, depth)
            right = table[k, :, 1].reshape(64, depth)
            halves = []
            for h in range(2):
                cols = pl.ds(h * half, half)
                halves.append(
                    jnp.dot(left, grads_v[0, :, cols], preferred_element_type=f32)
                    + jnp.dot(right, grads_v[1, :, cols], preferred_element_type=f32)
                )
            for q in range(8):
                both = [v[8 * q : 8 * q + 8] for v in halves]
                part[k, q] = jnp.concatenate(both, axis=0).astype(bf16)
            for d, q in peers:
                pltpu.make_async_remote_copy(
                    part.at[k, q], got.at[k, d - 1], b_send.at[k], b_recv.at[k],
                    (2 * q + core, j), MESH,
                ).start()

    def times(t, pr, dy, dx):
        from_chip = ((y + 4 - dy) % 4) * 2 + (x + 2 - dx) % 2
        block = 2 * from_chip + (core + pr) % 2
        return lax.dot_general(
            picked[t, pr, 4 * dx + dy], act_v[block], NT, preferred_element_type=f32
        )

    def arrive(n):
        d = NEAR[n][0] + 4 * NEAR[n][1]
        with scope("columns0_%d" % n):
            drain(picked.at[0, 0, d], a1_recv.at[d])
        pltpu.make_async_remote_copy(
            picked.at[0, 0, d], picked.at[0, 1, d], fw_send.at[0], fw_recv.at[d], sibling, MESH
        ).start()

    def sibling_arrive(n):
        d = ALL[n][0] + 4 * ALL[n][1]
        with scope("sibling_columns0"):
            drain(picked.at[0, 1, d], fw_recv.at[d])

    def to_mates(t, acc):
        with scope("to_mates%d" % t):
            k = 2 * t
            acc = acc.astype(bf16)
            proj[t, 0] = acc[:16]
            proj[t, 1] = acc[16:]
            pltpu.make_async_remote_copy(
                proj.at[t, 1 - core], table.at[k, member, core], sib_sem.at[t, 0], sib_sem.at[t, 1],
                sibling, MESH,
            ).start()
            for mate in mates:
                for to_core, to_dp in ((core, i), (1 - core, twin)):
                    pltpu.make_async_remote_copy(
                        proj.at[t, to_core], table.at[k, member, core], a2_send.at[k], a2_recv.at[k],
                        (to_dp, mate), MESH,
                    ).start()
            table[k, member, core] = proj[t, core]

    def to_others(t):
        with scope("to_others%d" % t):
            k = 2 * t
            drain(table.at[k, member, 1 - core], sib_sem.at[t, 1])
            for dz in (next_z, across):
                for to_lo in (0, 1):
                    pltpu.make_async_remote_copy(
                        table.at[k, member], table.at[k + 1, member], a2_send.at[k + 1],
                        a2_recv.at[k + 1], (i, at(dz, to_lo)), MESH,
                    ).start()

    acc = times(0, 0, 0, 0)
    for n, offset in enumerate(NEAR):
        arrive(n)
        if n == 0:
            send_columns(1)
        acc += times(0, 0, *offset)
        if n:
            sibling_arrive(n - 1)
            acc += times(0, 1, *ALL[n - 1])
    for n in (6, 7):
        sibling_arrive(n)
        acc += times(0, 1, *ALL[n])
    to_mates(0, acc)

    rest = pl.ds(1, 7)
    with scope("columns1"):
        drain(picked.at[1, 0, rest], a1_recv.at[8])
    pltpu.make_async_remote_copy(
        picked.at[1, 0, rest], picked.at[1, 1, rest], fw_send.at[1], fw_recv.at[8], sibling, MESH
    ).start()
    acc = times(1, 0, 0, 0)
    for offset in NEAR:
        acc += times(1, 0, *offset)
    total[...] = acc
    to_others(0)
    with scope("sibling_columns1"):
        drain(picked.at[1, 1], fw_recv.at[8])
    acc = total[...]
    for offset in ALL:
        acc += times(1, 1, *offset)
    to_mates(1, acc)

    for load in loads[1:]:
        load.wait()
    drain(grads_v.at[1 - core], og_sem.at[1])
    partial(0)
    to_others(1)

    def reduce(k):
        with scope("wait_sums%d" % k):
            drain(got.at[k], b_recv.at[k])
        with scope("adam%d" % k):
            low = part[k, chip].astype(f32)
            for d in range(7):
                low += got[k, d].astype(f32)
            mine = pl.ds(pl.multiple_of(8 * (2 * (k // 2) + (pair + k) % 2), 8), 8)
            rows = []
            for h in range(2):
                cols = pl.ds(h * half, half)
                g = low[8 * h : 8 * h + 8]
                nf = beta_one * first_v[mine, cols] + (1.0 - beta_one) * g
                ns = beta_two * second_v[mine, cols] + (1.0 - beta_two) * g * g
                new_first[mine, cols] = nf
                new_second[mine, cols] = ns
                rows.append(nf / first_fix / (jnp.sqrt(ns / second_fix) + adam_eps))
            send_v[k] = jnp.concatenate(rows, axis=0).astype(bf16)
            for d, q in peers:
                if d < 5 or RELAY[k] is None:
                    pltpu.make_async_remote_copy(
                        send_v.at[k], held.at[k, 0, d], c_send.at[k, 0], c_recv.at[k, slot_sem(d)],
                        (2 * q + core, j), MESH,
                    ).start()
            pltpu.make_async_remote_copy(
                send_v.at[k], held.at[k, 1, 0], cf_send.at[k], cs_recv.at[k], sibling, MESH
            ).start()
            pltpu.make_async_copy(send_v.at[k], held.at[k, 0, 0], out_sem.at[1]).start()

    def relay(k):
        if RELAY[k] == "y then x":
            with scope("wait_y_rows%d" % k):
                drain(held.at[k, 0, pl.ds(1, 3)], c_recv.at[k, 0])
            with scope("relay%d" % k):
                pltpu.make_async_remote_copy(
                    held.at[k, 0, pl.ds(1, 3)], held.at[k, 0, pl.ds(5, 3)], c_send.at[k, 1],
                    c_recv.at[k, 2], (2 * by_slot[4] + core, j), MESH,
                ).start()
        if RELAY[k] == "x then y":
            with scope("wait_x_rows%d" % k):
                drain(held.at[k, 0, 4], c_recv.at[k, 1])
            with scope("relay%d" % k):
                for d in (1, 3, 2):
                    pltpu.make_async_remote_copy(
                        held.at[k, 0, 4], held.at[k, 0, 4 + d], c_send.at[k, 1],
                        c_recv.at[k, 2], (2 * by_slot[d] + core, j), MESH,
                    ).start()

    def forward(k):
        with scope("wait_rows%d" % k):
            if RELAY[k] != "y then x":
                drain(held.at[k, 0, pl.ds(1, 3)], c_recv.at[k, 0])
            if RELAY[k] != "x then y":
                drain(held.at[k, 0, 4], c_recv.at[k, 1])
            drain(held.at[k, 0, pl.ds(5, 3)], c_recv.at[k, 2])
        others = pl.ds(1, 7)
        pltpu.make_async_remote_copy(
            held.at[k, 0, others], held.at[k, 1, others], cf_send.at[k], cf_recv.at[k],
            sibling, MESH,
        ).start()

    for k in range(1, 4):
        partial(k)
    reduce(0)
    for t in range(2):
        drain(picked.at[t, 0, pl.ds(0, 7)], a1_send.at[t])
        drain(picked.at[t, 1], fw_send.at[t])
        drain(proj.at[t, 0], sib_sem.at[t, 0])
    drain(grads, og_sem.at[0])
    reduce(1)
    for k in range(4):
        drain(table.at[k] if k % 2 else table.at[k, pl.ds(0, 3)], a2_send.at[k])
    reduce(2)
    relay(0)
    reduce(3)
    relay(1)
    relay(2)
    relay(3)
    for k in range(4):
        drain(got.at[k], b_send.at[k])
    outs = [
        mixed_out,
        pltpu.make_async_copy(new_first, first_o, out_sem.at[2]),
        pltpu.make_async_copy(new_second, second_o, out_sem.at[3]),
    ]
    for out in outs[1:]:
        out.start()
    for k in range(4):
        forward(k)

    for k in range(4):
        if RELAY[k] is None:
            drain(held.at[k, 0, pl.ds(1, 7)], c_send.at[k, 0])
        else:
            drain(held.at[k, 0, pl.ds(1, 4)], c_send.at[k, 0])
            drain(held.at[k, 0, pl.ds(5, 3)], c_send.at[k, 1])
        drain(held.at[k, 1], cf_send.at[k])
    for out in outs:
        out.wait()
    drain(send_v, out_sem.at[1])
    with scope("wait_sibling_rows"):
        for k in range(4):
            drain(held.at[k, 1, 0], cs_recv.at[k])
            drain(held.at[k, 1, pl.ds(1, 7)], cf_recv.at[k])


def finish(held, mixed, first_i, second_i, update, first_o, second_o, rows_v, update_v, sem):
    outs = [
        pltpu.make_async_copy(first_i, first_o, sem.at[0]),
        pltpu.make_async_copy(second_i, second_o, sem.at[1]),
    ]
    for out in outs:
        out.start()
    width = update.shape[1]
    half = width // 2
    done = 0
    for h in range(2):
        for k in range(4):
            rows = held[k].reshape(16, 16, half).astype(f32)[:, 8 * h : 8 * h + 8]
            rows_v[128 * k : 128 * k + 128, pl.ds(h * half, half)] = rows.reshape(128, half).astype(bf16)
        while done < width and done + 256 <= (h + 1) * half:
            cols = pl.ds(done, 256)
            update_v[:, cols] = jnp.dot(
                mixed[...], rows_v[:, cols], preferred_element_type=f32
            ).astype(bf16)
            out = pltpu.make_async_copy(update_v.at[:, cols], update.at[:, cols], sem.at[2 + done // 256])
            out.start()
            outs.append(out)
            done += 256
    with scope("results_out"):
        for out in outs:
            out.wait()


def on_device(act, basis, grads, first, second):
    tokens, depth = act.shape[0], basis.shape[0]
    rank, width = basis.shape[1], grads.shape[1]
    rows = first.shape[0]
    half = width // 2
    dma = pltpu.SemaphoreType.DMA
    anywhere = pl.BlockSpec(memory_space=pl.ANY)
    in_vmem = pl.BlockSpec(memory_space=pltpu.VMEM)
    operands = [pltpu.with_memory_space_constraint(v, pltpu.HBM) for v in (act, basis, grads, first, second)]
    held, mixed, new_first, new_second = pl.pallas_call(
        exchange,
        out_shape=(
            pltpu.VMEM((4, 2, 8, 16, half), bf16),
            pltpu.VMEM((depth, rank), bf16),
            pltpu.VMEM((rows, width), f32),
            pltpu.VMEM((rows, width), f32),
        ),
        in_specs=[anywhere] * 5,
        out_specs=[anywhere] * 4,
        scratch_shapes=[
            pltpu.VMEM((16, tokens, depth), bf16),
            pltpu.VMEM((depth, rank), bf16),
            pltpu.VMEM((2, tokens, width), bf16),
            pltpu.VMEM((rows, width), f32),
            pltpu.VMEM((rows, width), f32),
            pltpu.VMEM((depth, rank), bf16),
            pltpu.VMEM((2, 2, 8, 32, depth), bf16),
            pltpu.VMEM((2, 2, 16, tokens), bf16),
            pltpu.VMEM((4, 4, 2, 16, tokens), bf16),
            pltpu.VMEM((4, 8, 16, half), bf16),
            pltpu.VMEM((4, 7, 16, half), bf16),
            pltpu.VMEM((4, 16, half), bf16),
            pltpu.VMEM((32, tokens), f32),
            pltpu.VMEM((rows, width), f32),
            pltpu.VMEM((rows, width), f32),
            dma((5,)), dma((2,)), dma((2,)), dma((9,)), dma((2,)), dma((9,)), dma((2, 2)), dma((4,)), dma((4,)),
            dma((4,)), dma((4,)), dma((4, 2)), dma((4, 3)), dma((4,)), dma((4,)), dma((4,)),
            dma((4,)),
        ],
        compiler_params=pltpu.CompilerParams(
            collective_id=0, has_side_effects=True, vmem_limit_bytes=32 << 20
        ),
    )(*operands)
    return pl.pallas_call(
        finish,
        out_shape=(
            pltpu.HBM((depth, width), bf16),
            pltpu.HBM((rows, width), f32),
            pltpu.HBM((rows, width), f32),
        ),
        in_specs=[in_vmem, in_vmem, anywhere, anywhere],
        out_specs=[anywhere] * 3,
        scratch_shapes=[
            pltpu.VMEM((rank, width), bf16),
            pltpu.VMEM((depth, width), bf16),
            dma((2 + width // 256,)),
        ],
        compiler_params=pltpu.CompilerParams(vmem_limit_bytes=24 << 20),
    )(held, mixed, new_first, new_second)


def solution(mesh):
    placed = (P("dp", None), P("dp", None), P("dp", "tensor"), P("dp", "tensor"), P("dp", "tensor"))
    return jax.shard_map(
        on_device,
        mesh=mesh,
        in_specs=placed,
        out_specs=(P("dp", "tensor"), P("dp", "tensor"), P("dp", "tensor")),
        check_vma=False,
    )
```

time: 57.7 us -> 52.7 us (0.913)
  Pallas kernels: 56.9 us -> 51.9 us
    pallas_call x1, Pallas kernels: 54.8 us -> 49.8 us  [on_device(): pl.pallas_call(exchange, out_shape=(pltpu.VMEM((4, 2, 8, 16, half), bf16)...]
where the time goes in v3:
time: 52.7 us; the launch traced here: 52.6 us
  Pallas kernels  51.9 us (98%)
  between operations  0.64 us (1%)
    pallas_call x1, Pallas kernels, on_device(): pl.pallas_call(exchange, out_shape=(pltpu.VMEM((4, 2, 8, 16, half), bf16)...  49.8 us
    pallas_call x1, Pallas kernels, on_device(): pl.pallas_call(finish, out_shape=(pltpu.HBM((depth, width), bf16), pltpu....  2.08 us

profile of v3, /device:TPU:1, one launch (start us, length us, event | category | flops | bytes accessed | tf_op | source)
XLA Modules:
  0.0 52.6 jit_solution(14900451745370976449)
XLA Ops:
  0.6 49.8 %shard_map.76 = (bf16[4,2,8,16,896]{4,3,2,1,0:T(8,128)(2,1)S(1)}, bf16[512,512]{1,0:T(8,128)(2,1)S(1)}, f32[32,1792]{1,0:T(8,128)S(1)}, f32[32,1792]{1,0:T(8,128)S(1)}) custom-call(bf16[512,8192]{1,0:T(8,128)(2,1)} %act.1, bf16[512,512]{1,0:T(8,128)(2,1)} %basis.1, bf16[512,1792]{1,0:T(8,128)(2,1)} %grads.1, f32[32,1792]{1,0:T(8,128)} %first.1, ...), custom_call_target="tpu_custom_call" | custom-call | tf_op jit(solution)/shard_map/pallas_call | solution.py:376
  50.5 2.1 %shard_map.77 = (bf16[512,1792]{1,0:T(8,128)(2,1)}, f32[32,1792]{1,0:T(8,128)}, f32[32,1792]{1,0:T(8,128)}) custom-call(bf16[4,2,8,16,896]{4,3,2,1,0:T(8,128)(2,1)S(1)} %get-tuple-element.7.held, bf16[512,512]{1,0:T(8,128)(2,1)S(1)} %get-tuple-element.8.mixed, f32[32,1792]{1,0:T(8,128)S(1)} %get-tuple-element.9.first_i, ...), custom_call_target="tpu_custom_call" | custom-call | tf_op jit(solution)/shard_map/pallas_call | solution.py:410

commit v4 on v3

v4 whole, which is shorter than its diff:
```python
import jax
import jax.numpy as jnp
from jax import lax
from jax.experimental import pallas as pl
from jax.experimental.pallas import tpu as pltpu
from jax.sharding import PartitionSpec as P

beta_one = 0.9
beta_two = 0.999
first_fix = 1.0 - 0.9**50
second_fix = 1.0 - 0.999**50
adam_eps = 1e-08

MESH = pl.DeviceIdType.MESH
bf16 = jnp.bfloat16
f32 = jnp.float32
scope = jax.named_scope

NEAR = ((1, 0), (3, 0), (0, 1), (2, 0), (1, 1), (3, 1), (2, 1))
ALL = ((0, 0),) + NEAR
RELAY = ("y then x", "x then y", "y then x", None)
NT = (((1,), (1,)), ((), ()))


def drain(ref, sem):
    pltpu.make_async_copy(ref, ref, sem).wait()


def slot_sem(d):
    return 0 if d < 4 else 1 if d == 4 else 2


def exchange(
    act, basis, grads, first, second,
    held, mixed, early, new_first, new_second,
    act_v, basis_v, grads_v, first_v, second_v,
    picked, proj, table, part, got, total, rows_v,
    in_sem, sent, og_recv, a1_recv, fw_recv, sib_recv, a2_recv, b_recv, c_recv, cf_recv,
):
    i, j = lax.axis_index("dp"), lax.axis_index("tensor")
    core, chip = i % 2, i // 2
    y, x = chip // 2, chip % 2
    z, lo = j // 2, j % 2
    pair, odd = (z // 2) % 2, z % 2
    member = 2 * odd + lo
    depth = basis.shape[0]
    half = grads.shape[1] // 2
    twin = 2 * chip + (1 - core)

    sibling = (twin, j)
    peers = [(4 * dx + dy, ((y + dy) % 4) * 2 + (x + dx) % 2) for dy, dx in NEAR]
    by_slot = dict(peers)

    loads = [
        pltpu.make_async_copy(basis, basis_v, in_sem.at[0]),
        pltpu.make_async_copy(grads, grads_v.at[core], in_sem.at[1]),
        pltpu.make_async_copy(first, first_v, in_sem.at[2]),
        pltpu.make_async_copy(second, second_v, in_sem.at[3]),
    ]
    loads[0].start()

    barrier = pltpu.get_barrier_semaphore()
    def at(dz, to_lo):
        return 2 * ((z + 8 + dz) % 8) + to_lo

    mates = [at(0, 1 - lo), at(1 - 2 * odd, 0), at(1 - 2 * odd, 1)]
    next_z, across = 2 * odd - 1, 4 * lo - 2
    greeted = [sibling] + [(2 * q + core, j) for _, q in peers]
    greeted += [(to_dp, mate) for mate in mates for to_dp in (i, twin)]
    greeted += [(i, at(next_z, 0)), (i, at(next_z, 1)), (i, at(2, 0)), (i, at(-2, 1))]
    for device in greeted:
        pl.semaphore_signal(barrier, inc=1, device_id=device, device_id_type=MESH)

    loads[0].wait()
    r = lax.broadcasted_iota(jnp.int32, (64, 512), 0)
    col = lax.broadcasted_iota(jnp.int32, (64, 512), 1)
    owner = 2 * (2 * member + ((r >> 3) & 1)) + ((r >> 4) & 1)
    pick = (col == 32 * owner + 8 * (2 * (r >> 5) + pair) + (r & 7)).astype(bf16)
    both = lax.dot_general(pick, basis_v[...], NT, preferred_element_type=f32).astype(bf16)
    picked[0, 0, 0] = both[:32]
    picked[1, 0, 0] = both[32:]

    with scope("greet"):
        pl.semaphore_wait(barrier, len(greeted))

    def send_columns(t):
        with scope("send_columns%d" % t):
            for d, q in peers:
                pltpu.make_async_remote_copy(
                    picked.at[t, 0, 0], picked.at[t, 0, d], sent, a1_recv.at[8 if t else d],
                    (2 * q + core, j), MESH,
                ).start()
            pltpu.make_async_remote_copy(
                picked.at[t, 0, 0], picked.at[t, 1, 0], sent, fw_recv.at[8 * t], sibling, MESH
            ).start()

    send_columns(0)
    for b in range(16):
        pltpu.make_async_copy(act.at[:, pl.ds(b * depth, depth)], act_v.at[pl.ds(b * depth, depth)], in_sem.at[4]).start()
    for load in loads[1:]:
        load.start()
    pltpu.make_async_remote_copy(
        grads, grads_v.at[core], sent, og_recv, sibling, MESH
    ).start()

    with scope("reorder_basis"):
        row = lax.broadcasted_iota(jnp.int32, (512, 512), 0)
        s = lax.broadcasted_iota(jnp.int32, (512, 512), 1)
        k, pr, d, r = s >> 7, (s >> 6) & 1, (s >> 3) & 7, s & 7
        from_y = (y + 4 - (d & 3)) & 3
        from_x = (x + 2 - (d >> 2)) & 1
        from_core = (core + pr) & 1
        block = 2 * (k >> 1) + ((pair + k) & 1)
        col = 32 * (2 * (2 * from_y + from_x) + from_core) + 8 * block + r
        mix = (row == col).astype(bf16)
        mixed[...] = jnp.dot(basis_v[...], mix, preferred_element_type=f32).astype(bf16)

    with scope("act_wait"):
        pltpu.make_async_copy(act_v, act_v, in_sem.at[4]).wait()

    def partial(k):
        with scope("wait_projected%d" % k):
            drain(table.at[k] if k % 2 else table.at[k, pl.ds(0, 3)], a2_recv.at[k])
        with scope("partial%d" % k):
            left = table[k, :, 0].reshape(64, depth)
            right = table[k, :, 1].reshape(64, depth)
            halves = []
            for h in range(2):
                cols = pl.ds(h * half, half)
                halves.append(
                    jnp.dot(left, grads_v[0, :, cols], preferred_element_type=f32)
                    + jnp.dot(right, grads_v[1, :, cols], preferred_element_type=f32)
                )
            for q in range(8):
                both = [v[8 * q : 8 * q + 8] for v in halves]
                part[k, q] = jnp.concatenate(both, axis=0).astype(bf16)
            for d, q in peers:
                pltpu.make_async_remote_copy(
                    part.at[k, q], got.at[k, d - 1], sent, b_recv.at[k],
                    (2 * q + core, j), MESH,
                ).start()

    def times(t, pr, dy, dx):
        from_chip = ((y + 4 - dy) % 4) * 2 + (x + 2 - dx) % 2
        block = 2 * from_chip + (core + pr) % 2
        rows = act_v[pl.ds(pl.multiple_of(block * depth, depth), depth)]
        return lax.dot_general(picked[t, pr, 4 * dx + dy], rows, NT, preferred_element_type=f32)

    def arrive(n):
        d = NEAR[n][0] + 4 * NEAR[n][1]
        with scope("columns0_%d" % n):
            drain(picked.at[0, 0, d], a1_recv.at[d])
        pltpu.make_async_remote_copy(
            picked.at[0, 0, d], picked.at[0, 1, d], sent, fw_recv.at[d], sibling, MESH
        ).start()

    def sibling_arrive(n):
        d = ALL[n][0] + 4 * ALL[n][1]
        with scope("sibling_columns0"):
            drain(picked.at[0, 1, d], fw_recv.at[d])

    def to_mates(t, acc):
        with scope("to_mates%d" % t):
            k = 2 * t
            acc = acc.astype(bf16)
            proj[t, 0] = acc[:16]
            proj[t, 1] = acc[16:]
            pltpu.make_async_remote_copy(
                proj.at[t, 1 - core], table.at[k, member, core], sent, sib_recv.at[t],
                sibling, MESH,
            ).start()
            for mate in mates:
                for to_core, to_dp in ((core, i), (1 - core, twin)):
                    pltpu.make_async_remote_copy(
                        proj.at[t, to_core], table.at[k, member, core], sent, a2_recv.at[k],
                        (to_dp, mate), MESH,
                    ).start()
            table[k, member, core] = proj[t, core]

    def to_others(t):
        with scope("to_others%d" % t):
            k = 2 * t
            drain(table.at[k, member, 1 - core], sib_recv.at[t])
            for dz in (next_z, across):
                for to_lo in (0, 1):
                    pltpu.make_async_remote_copy(
                        table.at[k, member], table.at[k + 1, member], sent,
                        a2_recv.at[k + 1], (i, at(dz, to_lo)), MESH,
                    ).start()

    acc = times(0, 0, 0, 0)
    for n, offset in enumerate(NEAR):
        arrive(n)
        if n == 0:
            send_columns(1)
        acc += times(0, 0, *offset)
        if n:
            sibling_arrive(n - 1)
            acc += times(0, 1, *ALL[n - 1])
    for n in (6, 7):
        sibling_arrive(n)
        acc += times(0, 1, *ALL[n])
    to_mates(0, acc)

    rest = pl.ds(1, 7)
    with scope("columns1"):
        drain(picked.at[1, 0, rest], a1_recv.at[8])
    pltpu.make_async_remote_copy(
        picked.at[1, 0, rest], picked.at[1, 1, rest], sent, fw_recv.at[8], sibling, MESH
    ).start()
    acc = times(1, 0, 0, 0)
    for offset in NEAR:
        acc += times(1, 0, *offset)
    total[...] = acc
    to_others(0)
    with scope("sibling_columns1"):
        drain(picked.at[1, 1], fw_recv.at[8])
    acc = total[...]
    for offset in ALL:
        acc += times(1, 1, *offset)
    to_mates(1, acc)

    for load in loads[1:]:
        load.wait()
    drain(grads_v.at[1 - core], og_recv)
    partial(0)
    to_others(1)

    def reduce(k):
        with scope("wait_sums%d" % k):
            drain(got.at[k], b_recv.at[k])
        with scope("adam%d" % k):
            low = part[k, chip].astype(f32)
            for d in range(7):
                low += got[k, d].astype(f32)
            mine = pl.ds(pl.multiple_of(8 * (2 * (k // 2) + (pair + k) % 2), 8), 8)
            rows = []
            for h in range(2):
                cols = pl.ds(h * half, half)
                g = low[8 * h : 8 * h + 8]
                nf = beta_one * first_v[mine, cols] + (1.0 - beta_one) * g
                ns = beta_two * second_v[mine, cols] + (1.0 - beta_two) * g * g
                new_first[mine, cols] = nf
                new_second[mine, cols] = ns
                rows.append(nf / first_fix / (jnp.sqrt(ns / second_fix) + adam_eps))
            held[k, 0, 0] = jnp.concatenate(rows, axis=0).astype(bf16)
            for d, q in peers:
                if d < 5 or RELAY[k] is None:
                    pltpu.make_async_remote_copy(
                        held.at[k, 0, 0], held.at[k, 0, d], sent, c_recv.at[k, slot_sem(d)],
                        (2 * q + core, j), MESH,
                    ).start()
            pltpu.make_async_remote_copy(
                held.at[k, 0, 0], held.at[k, 1, 0], sent, cf_recv.at[k // 2], sibling, MESH
            ).start()

    def pass_on(k, which):
        slots = pl.ds(*((1, 3), (4, 1), (5, 3))[which])
        with scope("rows%d_%d" % (k, which)):
            drain(held.at[k, 0, slots], c_recv.at[k, which])
        pltpu.make_async_remote_copy(
            held.at[k, 0, slots], held.at[k, 1, slots], sent, cf_recv.at[k // 2], sibling, MESH
        ).start()

    def relay(k):
        if RELAY[k] == "y then x":
            pass_on(k, 0)
            pltpu.make_async_remote_copy(
                held.at[k, 0, pl.ds(1, 3)], held.at[k, 0, pl.ds(5, 3)], sent,
                c_recv.at[k, 2], (2 * by_slot[4] + core, j), MESH,
            ).start()
        if RELAY[k] == "x then y":
            pass_on(k, 1)
            for d in (1, 3, 2):
                pltpu.make_async_remote_copy(
                    held.at[k, 0, 4], held.at[k, 0, 4 + d], sent,
                    c_recv.at[k, 2], (2 * by_slot[d] + core, j), MESH,
                ).start()

    def in_order(k, h):
        rows = held[k].reshape(16, 16, half).astype(f32)[:, 8 * h : 8 * h + 8]
        return rows.reshape(128, half).astype(bf16)

    for k in range(1, 4):
        partial(k)
    reduce(0)
    reduce(1)
    reduce(2)
    relay(0)
    reduce(3)
    relay(1)
    relay(2)
    pass_on(0, 1)
    pass_on(0, 2)
    pass_on(1, 0)
    pass_on(1, 2)

    with scope("sibling_rows0"):
        drain(held.at[pl.ds(0, 2), 1], cf_recv.at[0])
    with scope("early_update"):
        for h in range(2):
            for k in range(2):
                rows_v[128 * k : 128 * k + 128, pl.ds(h * half, half)] = in_order(k, h)
        for t in range(2 * half // 256):
            cols = pl.ds(256 * t, 256)
            early[:, cols] = jnp.dot(
                mixed[:, pl.ds(0, 256)], rows_v[:, cols], preferred_element_type=f32
            )
    pass_on(3, 0)
    pass_on(3, 1)
    pass_on(2, 1)
    pass_on(2, 2)
    pass_on(3, 2)

    with scope("wait_sibling_rows"):
        drain(held.at[pl.ds(2, 2), 1], cf_recv.at[1])
    columns, rows = 32 * depth, 16 * half
    count = 2 * 15 * columns + depth * 2 * half + 14 * columns // 2 + 8 * columns + 4 * 22 * rows
    with scope("wait_sent"):
        drain(act_v.at[pl.ds(0, count // depth)], sent)


def finish(held, mixed, early, first_i, second_i, update, first_o, second_o, rows_v, update_v, sem):
    outs = [
        pltpu.make_async_copy(first_i, first_o, sem.at[0]),
        pltpu.make_async_copy(second_i, second_o, sem.at[1]),
    ]
    for out in outs:
        out.start()
    width = update.shape[1]
    half = width // 2
    done = 0
    for h in range(2):
        for k in range(2):
            rows = held[2 + k].reshape(16, 16, half).astype(f32)[:, 8 * h : 8 * h + 8]
            rows_v[128 * k : 128 * k + 128, pl.ds(h * half, half)] = rows.reshape(128, half).astype(bf16)
        while done < width and done + 256 <= (h + 1) * half:
            cols = pl.ds(done, 256)
            late = jnp.dot(mixed[:, pl.ds(256, 256)], rows_v[:, cols], preferred_element_type=f32)
            update_v[:, cols] = (early[:, cols] + late).astype(bf16)
            out = pltpu.make_async_copy(update_v.at[:, cols], update.at[:, cols], sem.at[2 + done // 256])
            out.start()
            outs.append(out)
            done += 256
    with scope("results_out"):
        for out in outs:
            out.wait()


def on_device(act, basis, grads, first, second):
    tokens, depth = act.shape[0], basis.shape[0]
    rank, width = basis.shape[1], grads.shape[1]
    rows = first.shape[0]
    half = width // 2
    dma = pltpu.SemaphoreType.DMA
    anywhere = pl.BlockSpec(memory_space=pl.ANY)
    in_vmem = pl.BlockSpec(memory_space=pltpu.VMEM)
    operands = [pltpu.with_memory_space_constraint(v, pltpu.HBM) for v in (act, basis, grads, first, second)]
    held, mixed, early, new_first, new_second = pl.pallas_call(
        exchange,
        out_shape=(
            pltpu.VMEM((4, 2, 8, 16, half), bf16),
            pltpu.VMEM((depth, rank), bf16),
            pltpu.VMEM((depth, width), f32),
            pltpu.VMEM((rows, width), f32),
            pltpu.VMEM((rows, width), f32),
        ),
        in_specs=[anywhere] * 5,
        out_specs=[in_vmem] * 5,
        scratch_shapes=[
            pltpu.VMEM((16 * tokens, depth), bf16),
            pltpu.VMEM((depth, rank), bf16),
            pltpu.VMEM((2, tokens, width), bf16),
            pltpu.VMEM((rows, width), f32),
            pltpu.VMEM((rows, width), f32),
            pltpu.VMEM((2, 2, 8, 32, depth), bf16),
            pltpu.VMEM((2, 2, 16, tokens), bf16),
            pltpu.VMEM((4, 4, 2, 16, tokens), bf16),
            pltpu.VMEM((4, 8, 16, half), bf16),
            pltpu.VMEM((4, 7, 16, half), bf16),
            pltpu.VMEM((32, tokens), f32),
            pltpu.VMEM((rank // 2, width), bf16),
            dma((5,)), dma, dma, dma((9,)), dma((9,)), dma((2,)), dma((4,)), dma((4,)),
            dma((4, 3)), dma((2,)),
        ],
        compiler_params=pltpu.CompilerParams(
            collective_id=0, has_side_effects=True, vmem_limit_bytes=32 << 20
        ),
    )(*operands)
    return pl.pallas_call(
        finish,
        out_shape=(
            pltpu.HBM((depth, width), bf16),
            pltpu.HBM((rows, width), f32),
            pltpu.HBM((rows, width), f32),
        ),
        in_specs=[in_vmem, in_vmem, in_vmem, anywhere, anywhere],
        out_specs=[anywhere] * 3,
        scratch_shapes=[
            pltpu.VMEM((rank // 2, width), bf16),
            pltpu.VMEM((depth, width), bf16),
            dma((2 + width // 256,)),
        ],
        compiler_params=pltpu.CompilerParams(vmem_limit_bytes=24 << 20),
    )(held, mixed, early, new_first, new_second)


def solution(mesh):
    placed = (P("dp", None), P("dp", None), P("dp", "tensor"), P("dp", "tensor"), P("dp", "tensor"))
    return jax.shard_map(
        on_device,
        mesh=mesh,
        in_specs=placed,
        out_specs=(P("dp", "tensor"), P("dp", "tensor"), P("dp", "tensor")),
        check_vma=False,
    )
```

time: 52.7 us -> 51.7 us (0.981)
  Pallas kernels: 51.9 us -> 51 us
where the time goes in v4:
time: 51.7 us; the launch traced here: 51.6 us
  Pallas kernels  51 us (99%)
  between operations  0.64 us (1%)
    pallas_call x1, Pallas kernels, on_device(): pl.pallas_call(exchange, out_shape=(pltpu.VMEM((4, 2, 8, 16, half), bf16)...  49.3 us
    pallas_call x1, Pallas kernels, on_device(): pl.pallas_call(finish, out_shape=(pltpu.HBM((depth, width), bf16), pltpu....  1.63 us

profile of v4, /device:TPU:1, one launch (start us, length us, event | category | flops | bytes accessed | tf_op | source)
XLA Modules:
  0.0 51.6 jit_solution(11593959080789971319)
XLA Ops:
  0.6 49.3 %shard_map.76 = (bf16[4,2,8,16,896]{4,3,2,1,0:T(8,128)(2,1)S(1)}, bf16[512,512]{1,0:T(8,128)(2,1)S(1)}, f32[512,1792]{1,0:T(8,128)S(1)}, f32[32,1792]{1,0:T(8,128)S(1)}, f32[32,1792]{1,0:T(8,128)S(1)}) custom-call(bf16[512,8192]{1,0:T(8,128)(2,1)} %act.1, bf16[512,512]{1,0:T(8,128)(2,1)} %basis.1, bf16[512,1792]{1,0:T(8,128)(2,1)} %grads.1, ...), custom_call_target="tpu_custom_call" | custom-call | tf_op jit(solution)/shard_map/pallas_call | solution.py:359
  50.0 1.6 %shard_map.77 = (bf16[512,1792]{1,0:T(8,128)(2,1)}, f32[32,1792]{1,0:T(8,128)}, f32[32,1792]{1,0:T(8,128)}) custom-call(bf16[4,2,8,16,896]{4,3,2,1,0:T(8,128)(2,1)S(1)} %get-tuple-element.8.held, bf16[512,512]{1,0:T(8,128)(2,1)S(1)} %get-tuple-element.9.mixed, f32[512,1792]{1,0:T(8,128)S(1)} %get-tuple-element.10.early, ...), custom_call_target="tpu_custom_call" | custom-call | tf_op jit(solution)/shard_map/pallas_call | solution.py:390

commit v5 on v4

--- a/solution.py
+++ b/solution.py
@@ -124,21 +124,23 @@
         with scope("partial%d" % k):
             left = table[k, :, 0].reshape(64, depth)
             right = table[k, :, 1].reshape(64, depth)
-            halves = []
-            for h in range(2):
-                cols = pl.ds(h * half, half)
-                halves.append(
-                    jnp.dot(left, grads_v[0, :, cols], preferred_element_type=f32)
-                    + jnp.dot(right, grads_v[1, :, cols], preferred_element_type=f32)
-                )
-            for q in range(8):
-                both = [v[8 * q : 8 * q + 8] for v in halves]
-                part[k, q] = jnp.concatenate(both, axis=0).astype(bf16)
-            for d, q in peers:
-                pltpu.make_async_remote_copy(
-                    part.at[k, q], got.at[k, d - 1], sent, b_recv.at[k],
-                    (2 * q + core, j), MESH,
-                ).start()
+            for start, size in ((0, 512), (512, half - 512)) if k == 0 else ((0, half),):
+                halves = []
+                for h in range(2):
+                    cols = pl.ds(h * half + start, size)
+                    halves.append(
+                        jnp.dot(left, grads_v[0, :, cols], preferred_element_type=f32)
+                        + jnp.dot(right, grads_v[1, :, cols], preferred_element_type=f32)
+                    )
+                piece = pl.ds(start, size)
+                for q in range(8):
+                    both = [v[8 * q : 8 * q + 8] for v in halves]
+                    part[k, q, :, piece] = jnp.concatenate(both, axis=0).astype(bf16)
+                for d, q in peers:
+                    pltpu.make_async_remote_copy(
+                        part.at[k, q, :, piece], got.at[k, d - 1, :, piece], sent, b_recv.at[k],
+                        (2 * q + core, j), MESH,
+                    ).start()
 
     def times(t, pr, dy, dx):
         from_chip = ((y + 4 - dy) % 4) * 2 + (x + 2 - dx) % 2
@@ -295,6 +297,9 @@
     pass_on(1, 0)
     pass_on(1, 2)
 
+    pass_on(2, 1)
+    pass_on(3, 0)
+
     with scope("sibling_rows0"):
         drain(held.at[pl.ds(0, 2), 1], cf_recv.at[0])
     with scope("early_update"):
@@ -306,9 +311,7 @@
             early[:, cols] = jnp.dot(
                 mixed[:, pl.ds(0, 256)], rows_v[:, cols], preferred_element_type=f32
             )
-    pass_on(3, 0)
     pass_on(3, 1)
-    pass_on(2, 1)
     pass_on(2, 2)
     pass_on(3, 2)
 

time: 51.7 us -> 51.7 us (level)
  no operation moved by 1% of the time
where the time goes in v5:
time: 51.7 us; the launch traced here: 51.6 us
  Pallas kernels  50.9 us (98%)
  between operations  0.64 us (1%)
    pallas_call x1, Pallas kernels, on_device(): pl.pallas_call(exchange, out_shape=(pltpu.VMEM((4, 2, 8, 16, half), bf16)...  49.3 us
    pallas_call x1, Pallas kernels, on_device(): pl.pallas_call(finish, out_shape=(pltpu.HBM((depth, width), bf16), pltpu....  1.63 us

profile of v5, /device:TPU:1, one launch (start us, length us, event | category | flops | bytes accessed | tf_op | source)
XLA Modules:
  0.0 51.6 jit_solution(3245189909027926204)
XLA Ops:
  0.6 49.3 %shard_map.76 = (bf16[4,2,8,16,896]{4,3,2,1,0:T(8,128)(2,1)S(1)}, bf16[512,512]{1,0:T(8,128)(2,1)S(1)}, f32[512,1792]{1,0:T(8,128)S(1)}, f32[32,1792]{1,0:T(8,128)S(1)}, f32[32,1792]{1,0:T(8,128)S(1)}) custom-call(bf16[512,8192]{1,0:T(8,128)(2,1)} %act.1, bf16[512,512]{1,0:T(8,128)(2,1)} %basis.1, bf16[512,1792]{1,0:T(8,128)(2,1)} %grads.1, ...), custom_call_target="tpu_custom_call" | custom-call | tf_op jit(solution)/shard_map/pallas_call | solution.py:362
  49.9 1.6 %shard_map.77 = (bf16[512,1792]{1,0:T(8,128)(2,1)}, f32[32,1792]{1,0:T(8,128)}, f32[32,1792]{1,0:T(8,128)}) custom-call(bf16[4,2,8,16,896]{4,3,2,1,0:T(8,128)(2,1)S(1)} %get-tuple-element.8.held, bf16[512,512]{1,0:T(8,128)(2,1)S(1)} %get-tuple-element.9.mixed, f32[512,1792]{1,0:T(8,128)S(1)} %get-tuple-element.10.early, ...), custom_call_target="tpu_custom_call" | custom-call | tf_op jit(solution)/shard_map/pallas_call | solution.py:393

commit v6 on v5

--- a/solution.py
+++ b/solution.py
@@ -332,19 +332,17 @@
         out.start()
     width = update.shape[1]
     half = width // 2
-    done = 0
     for h in range(2):
         for k in range(2):
             rows = held[2 + k].reshape(16, 16, half).astype(f32)[:, 8 * h : 8 * h + 8]
             rows_v[128 * k : 128 * k + 128, pl.ds(h * half, half)] = rows.reshape(128, half).astype(bf16)
-        while done < width and done + 256 <= (h + 1) * half:
-            cols = pl.ds(done, 256)
-            late = jnp.dot(mixed[:, pl.ds(256, 256)], rows_v[:, cols], preferred_element_type=f32)
-            update_v[:, cols] = (early[:, cols] + late).astype(bf16)
-            out = pltpu.make_async_copy(update_v.at[:, cols], update.at[:, cols], sem.at[2 + done // 256])
-            out.start()
-            outs.append(out)
-            done += 256
+    for t in range(update.shape[0] // 128):
+        at = pl.ds(128 * t, 128)
+        late = jnp.dot(mixed[at, pl.ds(256, 256)], rows_v[...], preferred_element_type=f32)
+        update_v[at] = (early[at] + late).astype(bf16)
+        out = pltpu.make_async_copy(update_v.at[at], update.at[at], sem.at[2 + t])
+        out.start()
+        outs.append(out)
     with scope("results_out"):
         for out in outs:
             out.wait()
@@ -402,7 +400,7 @@
         scratch_shapes=[
             pltpu.VMEM((rank // 2, width), bf16),
             pltpu.VMEM((depth, width), bf16),
-            dma((2 + width // 256,)),
+            dma((2 + depth // 128,)),
         ],
         compiler_params=pltpu.CompilerParams(vmem_limit_bytes=24 << 20),
     )(held, mixed, early, new_first, new_second)

time: 51.7 us -> 51.6 us (level)
  no operation moved by 1% of the time
where the time goes in v6:
time: 51.6 us; the launch traced here: 51.5 us
  Pallas kernels  50.9 us (99%)
  between operations  0.64 us (1%)
    pallas_call x1, Pallas kernels, on_device(): pl.pallas_call(exchange, out_shape=(pltpu.VMEM((4, 2, 8, 16, half), bf16)...  49.3 us
    pallas_call x1, Pallas kernels, on_device(): pl.pallas_call(finish, out_shape=(pltpu.HBM((depth, width), bf16), pltpu....  1.59 us

profile of v6, /device:TPU:1, one launch (start us, length us, event | category | flops | bytes accessed | tf_op | source)
XLA Modules:
  0.0 51.5 jit_solution(3059779640827961129)
XLA Ops:
  0.6 49.3 %shard_map.76 = (bf16[4,2,8,16,896]{4,3,2,1,0:T(8,128)(2,1)S(1)}, bf16[512,512]{1,0:T(8,128)(2,1)S(1)}, f32[512,1792]{1,0:T(8,128)S(1)}, f32[32,1792]{1,0:T(8,128)S(1)}, f32[32,1792]{1,0:T(8,128)S(1)}) custom-call(bf16[512,8192]{1,0:T(8,128)(2,1)} %act.1, bf16[512,512]{1,0:T(8,128)(2,1)} %basis.1, bf16[512,1792]{1,0:T(8,128)(2,1)} %grads.1, ...), custom_call_target="tpu_custom_call" | custom-call | tf_op jit(solution)/shard_map/pallas_call | solution.py:360
  49.9 1.6 %shard_map.77 = (bf16[512,1792]{1,0:T(8,128)(2,1)}, f32[32,1792]{1,0:T(8,128)}, f32[32,1792]{1,0:T(8,128)}) custom-call(bf16[4,2,8,16,896]{4,3,2,1,0:T(8,128)(2,1)S(1)} %get-tuple-element.8.held, bf16[512,512]{1,0:T(8,128)(2,1)S(1)} %get-tuple-element.9.mixed, f32[512,1792]{1,0:T(8,128)S(1)} %get-tuple-element.10.early, ...), custom_call_target="tpu_custom_call" | custom-call | tf_op jit(solution)/shard_map/pallas_call | solution.py:391
